TPU v7x, 128 devices: a whole 4x4x4 slice. The times are simulated.
128 devices in a mesh: dp: 16 (over x, y), tensor: 8 (over z, core).
Axes of the slice: x: 4, y: 4, z: 4, core: 2. Of those that a mesh axis runs over, the one named last changes fastest.
Arguments:
- query: bfloat16 [16384, 2048], P('dp', 'tensor'), may hold values from -26.25 to 26.25
- key: bfloat16 [16384, 512], P('dp'), may hold values from -26.25 to 26.25
- value: bfloat16 [16384, 512], P('dp'), may hold values from -6 to 6
- grad_out: bfloat16 [16384, 3584], P('dp'), may hold values from -12 to 12
- out_weight: bfloat16 [3584, 2048], P(None, 'tensor'), may hold values from -0.125 to 0.125
- plan: int32 [128], replicated, may hold values from 0 to 127, as said below
- segments: int32 [16384], P('dp'), may hold values from 0 to 1023, as said below
Outputs:
- grad_query: bfloat16 [16384, 2048], P('dp', 'tensor')
- grad_key: bfloat16 [16384, 512], P('dp')
- grad_value: bfloat16 [16384, 512], P('dp')
- grad_out_weight: float32 [3584, 2048], P('dp', 'tensor')
Inputs may be any that keep to these rules, and one draw needn't show every extreme that they name: plan is a permutation of the blocks; the 8 blocks that one index of dp holds go to 8 different indices of dp, at most one to each. `segments`: within each aligned block of 1024 rows of one index of dp the ids start at 0 and never fall; ids may skip values.
All inputs are finite; a program needn't handle non-finite values.
Results may differ from a plain program's by a relative error of at most 0.034.
The roundings to bfloat16 on the way count: a program that leaves them out, or rounds other values in their place, can miss the bound.
Values may be sent and summed in bfloat16 or wider, within the bound.
A program may use at most 128 MiB of HBM per device.

v0:
```python
import functools
import math

import jax
import jax.numpy as jnp
from jax import lax
from jax.experimental import pallas as pl
from jax.experimental.pallas import tpu as pltpu
from jax.sharding import PartitionSpec as P

D = 3584
KV = 4
HD = 128
HEADS = 16
RB = 128
NB = 8
RANKS = 16
LANES = 8
COLS = 256
TILE = 256
TILES = NB * RB // TILE
WROWS = D // RANKS

rope_base = 1000000.0
yarn_factor = 4.0
yarn_context = 32768.0
beta_fast = 32.0
beta_slow = 1.0
masked_score = -1e30
MESH = pl.DeviceIdType.MESH
BF = jnp.bfloat16
F32 = jnp.float32


def yarn_frequencies(head_size):
    half_size = head_size // 2

    def correction(rotations):
        return (
            head_size
            * math.log(yarn_context / (rotations * 2.0 * math.pi))
            / (2.0 * math.log(rope_base))
        )

    lower_bound = max(math.floor(correction(beta_fast)), 0)
    upper_bound = min(math.ceil(correction(beta_slow)), head_size - 1)
    ramp_span = max(upper_bound - lower_bound, 0.001)
    row_index = jnp.arange(half_size).astype(jnp.float32)
    extrap_freq = rope_base ** (-2.0 * row_index / head_size)
    interp_freq = extrap_freq / yarn_factor
    ramp_weight = jnp.clip((row_index - lower_bound) / ramp_span, 0.0, 1.0)
    return interp_freq * ramp_weight + extrap_freq * (1.0 - ramp_weight)


def dot(a, b, dims):
    return lax.dot_general(a, b, (dims, ((), ())), preferred_element_type=F32)


NN = ((1,), (0,))
NT = ((1,), (1,))
TN = ((0,), (0,))


def kernel(
    plan, seg, freq, q_hbm, k_hbm, v_hbm, g_hbm, w_hbm,
    gq_hbm, gk_hbm, gv_hbm, gw_hbm,
    q_v, kv_v, g_v, w_v, qkv_s, qkv_r, ga_v, ga_s, ga_r, kv2, qs, gas, outs, prob,
    ao_s, ao_r, dq_v, dq_s, dq_r, dkt, dvt, dkv_own, dkv_in, dkv_v, dkv_s, dkv_r,
    w_s, w_r, zk, aoh, gw_v, cosf, sinf, start,
    in_sem, g_sem, send_sem, recv_sem, pair_send, pair_recv, z_send, z_recv, out_sem,
):
    me = lax.axis_index("dp")
    lane = lax.axis_index("tensor")
    core = lax.rem(lane, 2)
    zed = lane // 2
    partner = lane + 1 - 2 * core
    inv_scale = 1.0 / math.sqrt(HD)
    log2_scale = inv_scale * math.log2(math.e)

    q_in = pltpu.make_async_copy(q_hbm, q_v, in_sem.at[0])
    q_in.start()
    head_cols = pl.ds(pl.multiple_of(zed * HD, HD), HD)
    k_in = pltpu.make_async_copy(k_hbm.at[:, :, head_cols], kv_v, in_sem.at[1])
    v_in = pltpu.make_async_copy(v_hbm.at[:, :, head_cols], kv_v, in_sem.at[1])
    pl.when(core == 0)(k_in.start)
    pl.when(core == 1)(v_in.start)
    w_in = pltpu.make_async_copy(w_hbm, w_v, in_sem.at[2])
    w_in.start()
    g_in = [
        pltpu.make_async_copy(
            g_hbm.at[pl.ds(2 * t, 2)], g_v.at[pl.ds(2 * t, 2)], g_sem.at[t]
        )
        for t in range(TILES)
    ]
    for copy in g_in:
        copy.start()

    barrier = pltpu.get_barrier_semaphore()

    def greet(o, carry):
        pl.semaphore_signal(
            barrier, inc=1, device_id={"dp": lax.rem(me + o, RANKS)}, device_id_type=MESH
        )
        return carry

    lax.fori_loop(1, RANKS, greet, 0)
    pl.semaphore_signal(barrier, inc=1, device_id={"tensor": partner}, device_id_type=MESH)
    for o in range(1, 4):
        peer = lax.rem(zed + o, 4) * 2 + core
        pl.semaphore_signal(barrier, inc=1, device_id={"tensor": peer}, device_id_type=MESH)

    def send_slot(dest):
        slot = jnp.int32(0)
        for b in range(NB):
            source = plan[dest * NB + b]
            slot = jnp.where((source >> 3) == me, source & 7, slot)
        return slot

    def back_slot(dest):
        slot = jnp.int32(0)
        for b in range(NB):
            slot = jnp.where((plan[me * NB + b] >> 3) == dest, b, slot)
        return slot

    def moved(stage, landing, kind, dest):
        return pltpu.make_async_remote_copy(
            src_ref=stage.at[dest],
            dst_ref=landing.at[me],
            send_sem=send_sem.at[kind],
            recv_sem=recv_sem.at[kind],
            device_id={"dp": dest},
            device_id_type=MESH,
        )

    def all_moved(stage, landing, kind):
        rest = pl.ds(0, RANKS - 1)
        return pltpu.make_async_remote_copy(
            src_ref=stage.at[rest],
            dst_ref=landing.at[rest],
            send_sem=send_sem.at[kind],
            recv_sem=recv_sem.at[kind],
            device_id={"dp": lax.rem(me + 1, RANKS)},
            device_id_type=MESH,
        )

    def exchange(fill, stage, landing, kind):
        def one(o, carry):
            dest = lax.rem(me + o, RANKS)
            fill(stage, dest, dest)
            moved(stage, landing, kind, dest).start()
            return carry

        lax.fori_loop(1, RANKS, one, 0)
        fill(landing, me, me)

    q_in.wait()
    pl.when(core == 0)(k_in.wait)
    pl.when(core == 1)(v_in.wait)
    pl.semaphore_wait(barrier, RANKS - 1 + 4)

    def fill_qkv(buffer, at, dest):
        slot = send_slot(dest)
        buffer[at, :, :COLS] = q_v[slot]
        buffer[at, :, COLS:] = kv_v[slot]

    exchange(fill_qkv, qkv_s, qkv_r, 0)

    w_in.wait()
    for t in range(TILES):
        g_in[t].wait()
    def project(t, carry):
        rows = pl.ds(2 * t, 2)
        product = dot(g_v[rows].reshape(TILE, D), w_v[...], NN)
        ga_v[rows] = product.astype(BF).reshape(2, RB, COLS)
        return carry

    lax.fori_loop(0, TILES, project, 0)

    def fill_ga(buffer, at, dest):
        buffer[at] = ga_v[send_slot(dest)]

    exchange(fill_ga, ga_s, ga_r, 1)

    factor = 0.1 * math.log(yarn_factor) + 1.0
    sign = jnp.where(lax.broadcasted_iota(jnp.int32, (1, RB), 1) < HD // 2, -factor, factor)
    for b in range(NB):
        mine = jnp.broadcast_to(seg[b : b + 1, :], (RB, RB)).T
        smaller = jnp.zeros((RB, RB), jnp.int32)
        for other in range(b + 1):
            smaller += jnp.where(seg[other : other + 1, :] < mine, 1, 0)
        first = jnp.sum(smaller, axis=1, keepdims=True)
        start[b] = jnp.broadcast_to(first, (RB, RB))

    def tables(b, carry):
        row = b * RB + lax.broadcasted_iota(jnp.int32, (RB, RB), 0)
        angle = (row - start[b]).astype(F32) * freq[0:1, :]
        cosf[b] = jnp.cos(angle) * factor
        sinf[b] = jnp.sin(angle) * sign
        return carry

    lax.fori_loop(0, NB, tables, 0)

    def find(g, carry):
        source = plan[g] - me * NB
        return tuple(jnp.where(source == j, g // NB, carry[j]) for j in range(NB))

    homes = lax.fori_loop(0, RANKS * NB, find, (jnp.int32(0),) * NB)

    def turned(x, cosine, sine):
        return x * cosine + pltpu.roll(x, HD // 2, 1) * sine

    def pair_copy(src, dst, i):
        return pltpu.make_async_remote_copy(
            src_ref=src, dst_ref=dst, send_sem=pair_send.at[i], recv_sem=pair_recv.at[i],
            device_id={"tensor": partner}, device_id_type=MESH,
        )

    all_moved(qkv_s, qkv_r, 0).wait_recv()
    is_key = (core == 0).astype(F32)

    def arrive_kv(b, carry):
        origin = plan[me * NB + b] >> 3
        x = qkv_r[origin][:, COLS:].astype(F32)
        cosine = cosf[b] * is_key + (1.0 - is_key)
        kv2[core, b] = turned(x, cosine, sinf[b] * is_key).astype(BF)
        return carry

    lax.fori_loop(0, NB, arrive_kv, 0)
    share_kv = pair_copy(kv2.at[core], kv2.at[core], 0)
    share_kv.start()

    for b in range(NB):
        block = qkv_r[plan[me * NB + b] >> 3]
        for h in range(2):
            x = block[:, h * HD : (h + 1) * HD].astype(F32)
            part = pl.ds((b % 2) * RB, RB)
            qs[b // 2 * 2 + h, part] = turned(x, cosf[b], sinf[b]).astype(BF)
    share_kv.wait_recv()

    def key_tile(kb):
        return kv2[0, 2 * kb : 2 * kb + 2].reshape(TILE, HD)

    def value_tile(kb):
        return kv2[1, 2 * kb : 2 * kb + 2].reshape(TILE, HD)

    column = lax.broadcasted_iota(jnp.int32, (TILE, TILE), 1)
    row_of = lax.broadcasted_iota(jnp.int32, (TILE, TILE), 0)
    for t in range(TILES):
        first = start[2 * t : 2 * t + 2].reshape(TILE, RB)
        first = jnp.concatenate([first, first], axis=1)

        def forward(h, carry):
            rows = qs[2 * t + h]
            scores = []
            for kb in range(t + 1):
                raw = dot(rows, key_tile(kb), NT)
                allowed = column + kb * TILE >= first
                if kb == t:
                    allowed = allowed & (column <= row_of)
                scores.append(jnp.where(allowed, raw, masked_score))
            peak = functools.reduce(jnp.maximum, scores)
            peak = jnp.max(peak, axis=1, keepdims=True)
            scores = [jnp.exp2((s - peak) * log2_scale) for s in scores]
            total = jnp.sum(functools.reduce(jnp.add, scores), axis=1, keepdims=True)
            share = 1.0 / total
            out = jnp.zeros((TILE, HD), F32)
            for kb in range(t + 1):
                p = scores[kb] * share
                prob[2 * t + h, :, kb * TILE : (kb + 1) * TILE] = p
                out += dot(p.astype(BF), value_tile(kb), NN)
            outs[2 * t : 2 * t + 2, h] = out.astype(BF).reshape(2, RB, HD)
            return carry

        lax.fori_loop(0, 2, forward, 0)

    def fill_out(buffer, at, dest):
        rows = outs[back_slot(dest)]
        for h in range(2):
            buffer[at, :, h * HD : (h + 1) * HD] = rows[h]

    exchange(fill_out, ao_s, ao_r, 2)

    all_moved(ga_s, ga_r, 1).wait_recv()
    for b in range(NB):
        block = ga_r[plan[me * NB + b] >> 3]
        for h in range(2):
            part = pl.ds((b % 2) * RB, RB)
            gas[b // 2 * 2 + h, part] = block[:, h * HD : (h + 1) * HD]

    dkt[...] = jnp.zeros_like(dkt)
    dvt[...] = jnp.zeros_like(dvt)
    for t in range(TILES):
        cosine = cosf[2 * t : 2 * t + 2].reshape(TILE, HD)
        sine = sinf[2 * t : 2 * t + 2].reshape(TILE, HD)

        def backward(h, carry):
            u = 2 * t + h
            upstream = gas[u]
            rows = qs[u]
            out = outs[2 * t : 2 * t + 2, h].reshape(TILE, HD)
            delta = jnp.sum(
                upstream.astype(F32) * out.astype(F32), axis=1, keepdims=True
            )
            dq = jnp.zeros((TILE, HD), F32)
            for kb in range(t + 1):
                cols = slice(kb * TILE, (kb + 1) * TILE)
                p = prob[u, :, cols]
                dp = dot(upstream, value_tile(kb), NT)
                ds = (p * (dp - delta)).astype(BF)
                dq += dot(ds, key_tile(kb), NN)
                dkt[:, cols] += dot(rows, ds, TN)
                dvt[:, cols] += dot(upstream, p.astype(BF), TN)
            dq = turned(dq * inv_scale, cosine, -sine).astype(BF)
            dq_v[2 * t : 2 * t + 2, h] = dq.reshape(2, RB, HD)
            return carry

        lax.fori_loop(0, 2, backward, 0)

    for b in range(NB):
        cols = slice(b * RB, (b + 1) * RB)
        dk = dkt[:, cols].T * inv_scale
        dkv_own[0, b] = turned(dk, cosf[b], -sinf[b]).astype(BF)
        dkv_own[1, b] = dvt[:, cols].T.astype(BF)
    share_dkv = pair_copy(dkv_own.at[1 - core], dkv_in, 1)
    share_dkv.start()

    def fill_dq(buffer, at, dest):
        rows = dq_v[back_slot(dest)]
        for h in range(2):
            buffer[at, :, h * HD : (h + 1) * HD] = rows[h]

    def fill_dkv(buffer, at, dest):
        buffer[at] = dkv_v[back_slot(dest)]

    share_dkv.wait_recv()
    for b in range(NB):
        dkv_v[b] = (dkv_own[core, b].astype(F32) + dkv_in[b].astype(F32)).astype(BF)
    exchange(fill_dkv, dkv_s, dkv_r, 3)
    exchange(fill_dq, dq_s, dq_r, 4)

    all_moved(ao_s, ao_r, 2).wait_recv()
    for j in range(NB):
        aoh[j * RB : (j + 1) * RB] = ao_r[homes[j]]
    chunk = 4 * WROWS
    for c in range(D // chunk):
        rows = g_v[:, :, c * chunk : (c + 1) * chunk].reshape(NB * RB, chunk)
        term = dot(aoh[...], rows, TN).T.astype(BF)
        for e in range(4):
            w_s[4 * c + e] = term[e * WROWS : (e + 1) * WROWS]

    def send_weight(o, carry):
        moved(w_s, w_r, 5, lax.rem(me + o, RANKS)).start()
        return carry

    lax.fori_loop(1, RANKS, send_weight, 0)
    w_r[me] = w_s[me]

    all_moved(dkv_s, dkv_r, 3).wait_recv()
    for j in range(NB):
        zk[core, zed, j] = dkv_r[homes[j]]
    z_copies = []
    for o in range(1, 4):
        copy = pltpu.make_async_remote_copy(
            src_ref=zk.at[core, zed], dst_ref=zk.at[core, zed],
            send_sem=z_send.at[o - 1], recv_sem=z_recv.at[o - 1],
            device_id={"tensor": lax.rem(zed + o, 4) * 2 + core}, device_id_type=MESH,
        )
        copy.start()
        z_copies.append(copy)

    all_moved(dq_s, dq_r, 4).wait_recv()
    for j in range(NB):
        q_v[j] = dq_r[homes[j]]
    gq_out = pltpu.make_async_copy(q_v, gq_hbm, out_sem.at[0])
    gq_out.start()

    for copy in z_copies:
        copy.wait_recv()
    share_z = pair_copy(zk.at[core], zk.at[core], 2)
    share_z.start()
    share_z.wait_recv()
    copies = []
    for k, target in enumerate((gk_hbm, gv_hbm)):
        for z in range(KV):
            copy = pltpu.make_async_copy(
                zk.at[k, z], target.at[:, :, z * HD : (z + 1) * HD], out_sem.at[1 + 4 * k + z]
            )
            copy.start()
            copies.append(copy)

    all_moved(w_s, w_r, 5).wait_recv()
    total = jnp.zeros((WROWS, COLS), F32)
    for r in range(RANKS):
        total += w_r[r].astype(F32)
    gw_v[...] = total * (1.0 / RANKS)
    gw_out = pltpu.make_async_copy(gw_v, gw_hbm, out_sem.at[9])
    gw_out.start()

    for kind, (stage, landing) in enumerate(
        ((qkv_s, qkv_r), (ga_s, ga_r), (ao_s, ao_r), (dkv_s, dkv_r), (dq_s, dq_r), (w_s, w_r))
    ):
        all_moved(stage, landing, kind).wait_send()
    share_kv.wait_send()
    share_dkv.wait_send()
    share_z.wait_send()
    for copy in z_copies:
        copy.wait_send()
    gq_out.wait()
    for copy in copies:
        copy.wait()
    gw_out.wait()


def local(query, key, value, grad_out, out_weight, plan, segments):
    blocked = (NB, RB)
    half = yarn_frequencies(HD)
    freq = jnp.broadcast_to(jnp.concatenate([half, half])[None, :], (8, HD))
    hbm = pl.BlockSpec(memory_space=pl.ANY)
    vmem = pl.BlockSpec(memory_space=pltpu.VMEM)
    V = pltpu.VMEM
    dma = pltpu.SemaphoreType.DMA
    rows = NB * RB
    gq, gk, gv, gw = pl.pallas_call(
        kernel,
        out_shape=(
            jax.ShapeDtypeStruct(blocked + (COLS,), BF),
            jax.ShapeDtypeStruct(blocked + (KV * HD,), BF),
            jax.ShapeDtypeStruct(blocked + (KV * HD,), BF),
            jax.ShapeDtypeStruct((WROWS, COLS), F32),
        ),
        in_specs=[pl.BlockSpec(memory_space=pltpu.SMEM), vmem, vmem] + [hbm] * 5,
        out_specs=(hbm,) * 4,
        scratch_shapes=[
            V(blocked + (COLS,), BF),
            V(blocked + (HD,), BF),
            V(blocked + (D,), BF),
            V((D, COLS), BF),
            V((RANKS, RB, COLS + HD), BF),
            V((RANKS, RB, COLS + HD), BF),
            V(blocked + (COLS,), BF),
            V((RANKS, RB, COLS), BF),
            V((RANKS, RB, COLS), BF),
            V((2,) + blocked + (HD,), BF),
            V((2 * TILES, TILE, HD), BF),
            V((2 * TILES, TILE, HD), BF),
            V((NB, 2, RB, HD), BF),
            V((2 * TILES, TILE, rows), F32),
            V((RANKS, RB, COLS), BF),
            V((RANKS, RB, COLS), BF),
            V((NB, 2, RB, HD), BF),
            V((RANKS, RB, COLS), BF),
            V((RANKS, RB, COLS), BF),
            V((HD, rows), F32),
            V((HD, rows), F32),
            V((2,) + blocked + (HD,), BF),
            V(blocked + (HD,), BF),
            V(blocked + (HD,), BF),
            V((RANKS, RB, HD), BF),
            V((RANKS, RB, HD), BF),
            V((RANKS, WROWS, COLS), BF),
            V((RANKS, WROWS, COLS), BF),
            V((2, KV) + blocked + (HD,), BF),
            V((rows, COLS), BF),
            V((WROWS, COLS), F32),
            V(blocked + (HD,), F32),
            V(blocked + (HD,), F32),
            V(blocked + (RB,), jnp.int32),
            dma((3,)),
            dma((TILES,)),
            dma((6,)),
            dma((6,)),
            dma((3,)),
            dma((3,)),
            dma((3,)),
            dma((3,)),
            dma((10,)),
        ],
        compiler_params=pltpu.CompilerParams(
            collective_id=0, has_side_effects=True, vmem_limit_bytes=60 * 2**20
        ),
        cost_estimate=pl.CostEstimate(
            flops=7 * 10**9, bytes_accessed=14 * 2**20, transcendentals=2 * 10**6
        ),
    )(
        plan,
        segments.reshape(NB, RB),
        freq,
        query.reshape(blocked + (COLS,)),
        key.reshape(blocked + (KV * HD,)),
        value.reshape(blocked + (KV * HD,)),
        grad_out.reshape(blocked + (D,)),
        out_weight,
    )
    return (
        gq.reshape(rows, COLS),
        gk.reshape(rows, KV * HD),
        gv.reshape(rows, KV * HD),
        gw,
    )


def solution(mesh):
    in_specs = (
        P("dp", "tensor"),
        P("dp", None),
        P("dp", None),
        P("dp", None),
        P(None, "tensor"),
        P(),
        P("dp"),
    )
    out_specs = (P("dp", "tensor"), P("dp", None), P("dp", None), P("dp", "tensor"))
    return jax.shard_map(local, mesh=mesh, in_specs=in_specs, out_specs=out_specs, check_vma=False)
```

profile of v0, /device:TPU:29, one launch (start us, length us, event | category | flops | bytes accessed | tf_op | source)
XLA Modules:
  0.0 117.2 jit_solution(14484469339753260425)
XLA Ops:
  0.6 0.1 pad_maximum_fusion
  0.7 0.6 broadcast_in_dim.2.freq
  1.3 107.8 %shard_map.102 = (bf16[8,128,256]{2,1,0:T(8,128)(2,1)}, bf16[8,128,512]{2,1,0:T(8,128)(2,1)}, bf16[8,128,512]{2,1,0:T(8,128)(2,1)}, f32[224,256]{1,0:T(8,128)}) custom-call(s32[128]{0:T(128)} %plan.1, s32[8,128]{1,0:T(8,128)} %bitcast.15, f32[8,128]{1,0:T(8,128)} %broadcast_in_dim.2.freq, bf16[8,128,256]{2,1,0:T(8,128)(2,1)} %bitcast.14, ...), custom_call_target="tpu_custom_call" | custom-call | flops 7000000000 | bytes 14680064 | tf_op jit(solution)/shard_map/pallas_call | solution.py:423
  109.2 1.9 %copy.15 = bf16[1024,256]{1,0:T(8,128)(2,1)} copy(bf16[1024,256]{1,0:T(8,128)(2,1)} %bitcast.10) | data formatting | bytes 1048576
  111.0 2.3 %copy.16 = bf16[1024,512]{1,0:T(8,128)(2,1)} copy(bf16[1024,512]{1,0:T(8,128)(2,1)} %bitcast.9) | data formatting | bytes 2097152
  113.3 2.3 %copy.17 = bf16[1024,512]{1,0:T(8,128)(2,1)} copy(bf16[1024,512]{1,0:T(8,128)(2,1)} %bitcast.8) | data formatting | bytes 2097152
  115.6 1.6 %copy.18 = f32[224,256]{1,0:T(8,128)} copy(f32[224,256]{1,0:T(8,128)} %get-tuple-element.19) | data formatting | bytes 458752
  (1 shorter events, 0.0 us)
where the time goes:
time: 118 us; the launch traced here: 117 us
  Pallas kernels  108 us (92%)
  local copies, waits for them, and re-layouts  8.63 us (7%)
    pallas_call x1, Pallas kernels, local(): pl.pallas_call(kernel, out_shape=(jax.ShapeDtypeStruct(blocked + (COLS,),...  108 us
    unnamed x4, local copies, waits for them, and re-layouts  8.03 us

commit v1 on v0

--- a/solution.py
+++ b/solution.py
@@ -3,6 +3,7 @@
 
 import jax
 import jax.numpy as jnp
+import numpy as np
 from jax import lax
 from jax.experimental import pallas as pl
 from jax.experimental.pallas import tpu as pltpu
@@ -20,6 +21,13 @@
 TILE = 256
 TILES = NB * RB // TILE
 WROWS = D // RANKS
+SIDE = 4
+ORDER = (
+    (1, 0), (0, 1), (3, 0), (0, 3), (2, 0), (0, 2), (1, 1), (3, 3),
+    (1, 3), (3, 1), (2, 2), (1, 2), (2, 1), (3, 2), (2, 3),
+)
+DX = sum(dx << (2 * i) for i, (dx, dy) in enumerate(ORDER))
+DY = sum(dy << (2 * i) for i, (dx, dy) in enumerate(ORDER))
 
 rope_base = 1000000.0
 yarn_factor = 4.0
@@ -45,10 +53,10 @@
     lower_bound = max(math.floor(correction(beta_fast)), 0)
     upper_bound = min(math.ceil(correction(beta_slow)), head_size - 1)
     ramp_span = max(upper_bound - lower_bound, 0.001)
-    row_index = jnp.arange(half_size).astype(jnp.float32)
+    row_index = np.arange(half_size).astype(np.float64)
     extrap_freq = rope_base ** (-2.0 * row_index / head_size)
     interp_freq = extrap_freq / yarn_factor
-    ramp_weight = jnp.clip((row_index - lower_bound) / ramp_span, 0.0, 1.0)
+    ramp_weight = np.clip((row_index - lower_bound) / ramp_span, 0.0, 1.0)
     return interp_freq * ramp_weight + extrap_freq * (1.0 - ramp_weight)
 
 
@@ -66,16 +74,32 @@
     gq_hbm, gk_hbm, gv_hbm, gw_hbm,
     q_v, kv_v, g_v, w_v, qkv_s, qkv_r, ga_v, ga_s, ga_r, kv2, qs, gas, outs, prob,
     ao_s, ao_r, dq_v, dq_s, dq_r, dkt, dvt, dkv_own, dkv_in, dkv_v, dkv_s, dkv_r,
-    w_s, w_r, zk, aoh, gw_v, cosf, sinf, start,
-    in_sem, g_sem, send_sem, recv_sem, pair_send, pair_recv, z_send, z_recv, out_sem,
+    w_s, w_r, w2_s, w2_r, zk, aoh, gw_v, cosf, sinf, start,
+    in_sem, g_sem, send_sem, recv_sem, pair_send, pair_recv, z_send, z_recv, w_send, w_recv, out_sem,
 ):
     me = lax.axis_index("dp")
     lane = lax.axis_index("tensor")
     core = lax.rem(lane, 2)
     zed = lane // 2
     partner = lane + 1 - 2 * core
+    my_x = me // SIDE
+    my_y = lax.rem(me, SIDE)
     inv_scale = 1.0 / math.sqrt(HD)
     log2_scale = inv_scale * math.log2(math.e)
+
+    barrier = pltpu.get_barrier_semaphore()
+
+    def greet(o, carry):
+        pl.semaphore_signal(
+            barrier, inc=1, device_id={"dp": lax.rem(me + o, RANKS)}, device_id_type=MESH
+        )
+        return carry
+
+    lax.fori_loop(1, RANKS, greet, 0)
+    pl.semaphore_signal(barrier, inc=1, device_id={"tensor": partner}, device_id_type=MESH)
+    for o in range(1, 4):
+        peer = lax.rem(zed + o, 4) * 2 + core
+        pl.semaphore_signal(barrier, inc=1, device_id={"tensor": peer}, device_id_type=MESH)
 
     q_in = pltpu.make_async_copy(q_hbm, q_v, in_sem.at[0])
     q_in.start()
@@ -95,20 +119,6 @@
     for copy in g_in:
         copy.start()
 
-    barrier = pltpu.get_barrier_semaphore()
-
-    def greet(o, carry):
-        pl.semaphore_signal(
-            barrier, inc=1, device_id={"dp": lax.rem(me + o, RANKS)}, device_id_type=MESH
-        )
-        return carry
-
-    lax.fori_loop(1, RANKS, greet, 0)
-    pl.semaphore_signal(barrier, inc=1, device_id={"tensor": partner}, device_id_type=MESH)
-    for o in range(1, 4):
-        peer = lax.rem(zed + o, 4) * 2 + core
-        pl.semaphore_signal(barrier, inc=1, device_id={"tensor": peer}, device_id_type=MESH)
-
     def send_slot(dest):
         slot = jnp.int32(0)
         for b in range(NB):
@@ -145,12 +155,15 @@
 
     def exchange(fill, stage, landing, kind):
         def one(o, carry):
-            dest = lax.rem(me + o, RANKS)
+            dxs, dys = carry
+            x = lax.rem(my_x + lax.rem(dxs, SIDE), SIDE)
+            y = lax.rem(my_y + lax.rem(dys, SIDE), SIDE)
+            dest = x * SIDE + y
             fill(stage, dest, dest)
             moved(stage, landing, kind, dest).start()
-            return carry
-
-        lax.fori_loop(1, RANKS, one, 0)
+            return dxs // SIDE, dys // SIDE
+
+        lax.fori_loop(1, RANKS, one, (jnp.int32(DX), jnp.int32(DY)))
         fill(landing, me, me)
 
     q_in.wait()
@@ -336,24 +349,38 @@
     for b in range(NB):
         dkv_v[b] = (dkv_own[core, b].astype(F32) + dkv_in[b].astype(F32)).astype(BF)
     exchange(fill_dkv, dkv_s, dkv_r, 3)
-    exchange(fill_dq, dq_s, dq_r, 4)
 
     all_moved(ao_s, ao_r, 2).wait_recv()
     for j in range(NB):
         aoh[j * RB : (j + 1) * RB] = ao_r[homes[j]]
-    chunk = 4 * WROWS
-    for c in range(D // chunk):
+    chunk = SIDE * WROWS
+    for c in range(SIDE):
         rows = g_v[:, :, c * chunk : (c + 1) * chunk].reshape(NB * RB, chunk)
         term = dot(aoh[...], rows, TN).T.astype(BF)
-        for e in range(4):
-            w_s[4 * c + e] = term[e * WROWS : (e + 1) * WROWS]
-
-    def send_weight(o, carry):
-        moved(w_s, w_r, 5, lax.rem(me + o, RANKS)).start()
-        return carry
-
-    lax.fori_loop(1, RANKS, send_weight, 0)
-    w_r[me] = w_s[me]
+        for e in range(SIDE):
+            part = term[e * WROWS : (e + 1) * WROWS]
+            w_s[0, c, e] = part[:, :HD]
+            w_s[1, e, c] = part[:, HD:]
+
+    mine = (my_x, my_y)
+
+    def along(half, step, o):
+        axis = half if step == 0 else 1 - half
+        to = lax.rem(mine[axis] + o, SIDE)
+        dest = to * SIDE + my_y if axis == 0 else my_x * SIDE + to
+        stage, landing = ((w_s, w_r), (w2_s, w2_r))[step]
+        return pltpu.make_async_remote_copy(
+            src_ref=stage.at[half, to], dst_ref=landing.at[half, mine[axis]],
+            send_sem=w_send.at[step, half, o - 1], recv_sem=w_recv.at[step, half, o - 1],
+            device_id={"dp": dest}, device_id_type=MESH,
+        )
+
+    w_copies = [[along(half, step, o) for o in (1, 3, 2) for half in range(2)] for step in range(2)]
+    for copy in w_copies[0]:
+        copy.start()
+    for half in range(2):
+        w_r[half, mine[half]] = w_s[half, mine[half]]
+    exchange(fill_dq, dq_s, dq_r, 4)
 
     all_moved(dkv_s, dkv_r, 3).wait_recv()
     for j in range(NB):
@@ -367,6 +394,19 @@
         )
         copy.start()
         z_copies.append(copy)
+
+    for copy in w_copies[0]:
+        copy.wait_recv()
+    for half in range(2):
+        for e in range(SIDE):
+            total = jnp.zeros((WROWS, HD), F32)
+            for r in range(SIDE):
+                total += w_r[half, r, e].astype(F32)
+            w2_s[half, e] = total.astype(BF)
+    for copy in w_copies[1]:
+        copy.start()
+    for half in range(2):
+        w2_r[half, mine[1 - half]] = w2_s[half, mine[1 - half]]
 
     all_moved(dq_s, dq_r, 4).wait_recv()
     for j in range(NB):
@@ -388,18 +428,22 @@
             copy.start()
             copies.append(copy)
 
-    all_moved(w_s, w_r, 5).wait_recv()
-    total = jnp.zeros((WROWS, COLS), F32)
-    for r in range(RANKS):
-        total += w_r[r].astype(F32)
-    gw_v[...] = total * (1.0 / RANKS)
+    for copy in w_copies[1]:
+        copy.wait_recv()
+    for half in range(2):
+        total = jnp.zeros((WROWS, HD), F32)
+        for r in range(SIDE):
+            total += w2_r[half, r].astype(F32)
+        gw_v[:, half * HD : (half + 1) * HD] = total * (1.0 / RANKS)
     gw_out = pltpu.make_async_copy(gw_v, gw_hbm, out_sem.at[9])
     gw_out.start()
 
     for kind, (stage, landing) in enumerate(
-        ((qkv_s, qkv_r), (ga_s, ga_r), (ao_s, ao_r), (dkv_s, dkv_r), (dq_s, dq_r), (w_s, w_r))
+        ((qkv_s, qkv_r), (ga_s, ga_r), (ao_s, ao_r), (dkv_s, dkv_r), (dq_s, dq_r))
     ):
         all_moved(stage, landing, kind).wait_send()
+    for copy in w_copies[0] + w_copies[1]:
+        copy.wait_send()
     share_kv.wait_send()
     share_dkv.wait_send()
     share_z.wait_send()
@@ -411,10 +455,33 @@
     gw_out.wait()
 
 
+def hand_on(*refs):
+    source, target, held, sems = refs[:4], refs[4:8], refs[8:12], refs[12]
+    parts = []
+    for k in range(4):
+        half = source[k].shape[0] // 2
+        for h in range(2):
+            part = pl.ds(h * half, half)
+            sem = sems.at[2 * k + h]
+            parts.append(
+                (
+                    pltpu.make_async_copy(source[k].at[part], held[k].at[part], sem),
+                    pltpu.make_async_copy(held[k].at[part], target[k].at[part], sem),
+                )
+            )
+    for load, store in parts:
+        load.start()
+    for load, store in parts:
+        load.wait()
+        store.start()
+    for load, store in parts:
+        store.wait()
+
+
 def local(query, key, value, grad_out, out_weight, plan, segments):
     blocked = (NB, RB)
     half = yarn_frequencies(HD)
-    freq = jnp.broadcast_to(jnp.concatenate([half, half])[None, :], (8, HD))
+    freq = np.tile(np.concatenate([half, half]), (8, 1)).astype(np.float32)
     hbm = pl.BlockSpec(memory_space=pl.ANY)
     vmem = pl.BlockSpec(memory_space=pltpu.VMEM)
     V = pltpu.VMEM
@@ -457,8 +524,10 @@
             V(blocked + (HD,), BF),
             V((RANKS, RB, HD), BF),
             V((RANKS, RB, HD), BF),
-            V((RANKS, WROWS, COLS), BF),
-            V((RANKS, WROWS, COLS), BF),
+            V((2, SIDE, SIDE, WROWS, HD), BF),
+            V((2, SIDE, SIDE, WROWS, HD), BF),
+            V((2, SIDE, WROWS, HD), BF),
+            V((2, SIDE, WROWS, HD), BF),
             V((2, KV) + blocked + (HD,), BF),
             V((rows, COLS), BF),
             V((WROWS, COLS), F32),
@@ -467,12 +536,14 @@
             V(blocked + (RB,), jnp.int32),
             dma((3,)),
             dma((TILES,)),
-            dma((6,)),
-            dma((6,)),
+            dma((5,)),
+            dma((5,)),
             dma((3,)),
             dma((3,)),
             dma((3,)),
             dma((3,)),
+            dma((2, 2, 3)),
+            dma((2, 2, 3)),
             dma((10,)),
         ],
         compiler_params=pltpu.CompilerParams(
@@ -491,6 +562,13 @@
         grad_out.reshape(blocked + (D,)),
         out_weight,
     )
+    gq, gk, gv, gw = pl.pallas_call(
+        hand_on,
+        out_shape=tuple(jax.ShapeDtypeStruct(x.shape, x.dtype) for x in (gq, gk, gv, gw)),
+        in_specs=[hbm] * 4,
+        out_specs=(hbm,) * 4,
+        scratch_shapes=[V(x.shape, x.dtype) for x in (gq, gk, gv, gw)] + [dma((8,))],
+    )(gq, gk, gv, gw)
     return (
         gq.reshape(rows, COLS),
         gk.reshape(rows, KV * HD),

time: 118 us -> 89.5 us (0.76)
  the two profiles are of different devices: /device:TPU:29 before, /device:TPU:1 now
where the time goes in v1:
time: 89.5 us; the launch traced here: 88.2 us
  Pallas kernels  87.6 us (98%)
    pallas_call x1, Pallas kernels, local(): pl.pallas_call(kernel, out_shape=(jax.ShapeDtypeStruct(blocked + (COLS,),...  84.9 us
    pallas_call x1, Pallas kernels, local(): pl.pallas_call(hand_on, out_shape=tuple((jax.ShapeDtypeStruct(x.shape, x....  2.65 us

profile of v1, /device:TPU:1, one launch (start us, length us, event | category | flops | bytes accessed | tf_op | source)
XLA Modules:
  0.0 88.2 jit_solution(10535945623262851855)
XLA Ops:
  0.6 84.9 %shard_map.111 = (bf16[8,128,256]{2,1,0:T(8,128)(2,1)}, bf16[8,128,512]{2,1,0:T(8,128)(2,1)}, bf16[8,128,512]{2,1,0:T(8,128)(2,1)}, f32[224,256]{1,0:T(8,128)}) custom-call(s32[128]{0:T(128)} %plan.1, s32[8,128]{1,0:T(8,128)} %bitcast.15, f32[8,128]{1,0:T(8,128)} %constant.2.clone.freq, bf16[8,128,256]{2,1,0:T(8,128)(2,1)} %bitcast.13, ...), custom_call_target="tpu_custom_call" | custom-call | flops 7000000000 | bytes 14680064 | tf_op jit(solution)/shard_map/pallas_call | solution.py:490
  85.6 2.6 %shard_map.112 = (bf16[8,128,256]{2,1,0:T(8,128)(2,1)}, bf16[8,128,512]{2,1,0:T(8,128)(2,1)}, bf16[8,128,512]{2,1,0:T(8,128)(2,1)}, f32[224,256]{1,0:T(8,128)}) custom-call(bf16[8,128,256]{2,1,0:T(8,128)(2,1)} %get-tuple-element.12.refs_0_, bf16[8,128,512]{2,1,0:T(8,128)(2,1)} %get-tuple-element.13.refs_1_, bf16[8,128,512]{2,1,0:T(8,128)(2,1)} %get-tuple-element.14.refs_2_, ...), custom_call_target="tpu_custom_call" | custom-call | tf_op jit(solution)/shard_map/pallas_call | solution.py:565

commit v2 on v1

--- a/solution.py
+++ b/solution.py
@@ -23,8 +23,8 @@
 WROWS = D // RANKS
 SIDE = 4
 ORDER = (
-    (1, 0), (0, 1), (3, 0), (0, 3), (2, 0), (0, 2), (1, 1), (3, 3),
-    (1, 3), (3, 1), (2, 2), (1, 2), (2, 1), (3, 2), (2, 3),
+    (1, 0), (0, 1), (3, 3), (2, 0), (0, 3), (1, 1), (3, 0), (0, 2),
+    (1, 3), (3, 1), (2, 2), (1, 2), (2, 3), (3, 2), (2, 1),
 )
 DX = sum(dx << (2 * i) for i, (dx, dy) in enumerate(ORDER))
 DY = sum(dy << (2 * i) for i, (dx, dy) in enumerate(ORDER))
@@ -72,7 +72,7 @@
 def kernel(
     plan, seg, freq, q_hbm, k_hbm, v_hbm, g_hbm, w_hbm,
     gq_hbm, gk_hbm, gv_hbm, gw_hbm,
-    q_v, kv_v, g_v, w_v, qkv_s, qkv_r, ga_v, ga_s, ga_r, kv2, qs, gas, outs, prob,
+    q_v, kv_v, g_v, w_v, q_s, q_r, kv_s, kv_r, ga_v, ga_s, ga_r, kv2, qs, gas, outs, prob,
     ao_s, ao_r, dq_v, dq_s, dq_r, dkt, dvt, dkv_own, dkv_in, dkv_v, dkv_s, dkv_r,
     w_s, w_r, w2_s, w2_r, zk, aoh, gw_v, cosf, sinf, start,
     in_sem, g_sem, send_sem, recv_sem, pair_send, pair_recv, z_send, z_recv, w_send, w_recv, out_sem,
@@ -132,10 +132,10 @@
             slot = jnp.where((plan[me * NB + b] >> 3) == dest, b, slot)
         return slot
 
-    def moved(stage, landing, kind, dest):
+    def moved(stage, landing, kind, dest, h):
         return pltpu.make_async_remote_copy(
-            src_ref=stage.at[dest],
-            dst_ref=landing.at[me],
+            src_ref=stage.at[dest, pl.ds(64 * h, 64)],
+            dst_ref=landing.at[me, pl.ds(64 * h, 64)],
             send_sem=send_sem.at[kind],
             recv_sem=recv_sem.at[kind],
             device_id={"dp": dest},
@@ -153,30 +153,40 @@
             device_id_type=MESH,
         )
 
-    def exchange(fill, stage, landing, kind):
+    def round_of(stage, landing, kind, half, fill):
         def one(o, carry):
             dxs, dys = carry
             x = lax.rem(my_x + lax.rem(dxs, SIDE), SIDE)
             y = lax.rem(my_y + lax.rem(dys, SIDE), SIDE)
             dest = x * SIDE + y
-            fill(stage, dest, dest)
-            moved(stage, landing, kind, dest).start()
+            if half == 0:
+                fill(stage, dest, dest)
+            moved(stage, landing, kind, dest, half).start()
             return dxs // SIDE, dys // SIDE
 
-        lax.fori_loop(1, RANKS, one, (jnp.int32(DX), jnp.int32(DY)))
-        fill(landing, me, me)
-
-    q_in.wait()
+        lax.fori_loop(1, RANKS, one, (DX + core * (DY - DX), DY + core * (DX - DY)))
+        if half == 0:
+            fill(landing, me, me)
+
+    def exchange(fill, stage, landing, kind):
+        for half in range(2):
+            round_of(stage, landing, kind, half, fill)
+
     pl.when(core == 0)(k_in.wait)
     pl.when(core == 1)(v_in.wait)
     pl.semaphore_wait(barrier, RANKS - 1 + 4)
 
-    def fill_qkv(buffer, at, dest):
-        slot = send_slot(dest)
-        buffer[at, :, :COLS] = q_v[slot]
-        buffer[at, :, COLS:] = kv_v[slot]
-
-    exchange(fill_qkv, qkv_s, qkv_r, 0)
+    def fill_kv(buffer, at, dest):
+        buffer[at] = kv_v[send_slot(dest)]
+
+    exchange(fill_kv, kv_s, kv_r, 5)
+
+    q_in.wait()
+
+    def fill_q(buffer, at, dest):
+        buffer[at] = q_v[send_slot(dest)]
+
+    exchange(fill_q, q_s, q_r, 0)
 
     w_in.wait()
     for t in range(TILES):
@@ -228,12 +238,12 @@
             device_id={"tensor": partner}, device_id_type=MESH,
         )
 
-    all_moved(qkv_s, qkv_r, 0).wait_recv()
+    all_moved(kv_s, kv_r, 5).wait_recv()
     is_key = (core == 0).astype(F32)
 
     def arrive_kv(b, carry):
         origin = plan[me * NB + b] >> 3
-        x = qkv_r[origin][:, COLS:].astype(F32)
+        x = kv_r[origin].astype(F32)
         cosine = cosf[b] * is_key + (1.0 - is_key)
         kv2[core, b] = turned(x, cosine, sinf[b] * is_key).astype(BF)
         return carry
@@ -242,8 +252,9 @@
     share_kv = pair_copy(kv2.at[core], kv2.at[core], 0)
     share_kv.start()
 
+    all_moved(q_s, q_r, 0).wait_recv()
     for b in range(NB):
-        block = qkv_r[plan[me * NB + b] >> 3]
+        block = q_r[plan[me * NB + b] >> 3]
         for h in range(2):
             x = block[:, h * HD : (h + 1) * HD].astype(F32)
             part = pl.ds((b % 2) * RB, RB)
@@ -364,23 +375,35 @@
 
     mine = (my_x, my_y)
 
-    def along(half, step, o):
+    def along(half, step, o, e):
         axis = half if step == 0 else 1 - half
         to = lax.rem(mine[axis] + o, SIDE)
         dest = to * SIDE + my_y if axis == 0 else my_x * SIDE + to
+        if step == 0:
+            src, dst = w_s.at[half, to, e], w_r.at[half, mine[axis], e]
+        else:
+            src, dst = w2_s.at[half, to], w2_r.at[half, mine[axis]]
+        return pltpu.make_async_remote_copy(
+            src_ref=src, dst_ref=dst, send_sem=w_send.at[step, half], recv_sem=w_recv.at[step, half],
+            device_id={"dp": dest}, device_id_type=MESH,
+        )
+
+    def all_along(half, step):
         stage, landing = ((w_s, w_r), (w2_s, w2_r))[step]
+        rest = pl.ds(0, SIDE - 1)
         return pltpu.make_async_remote_copy(
-            src_ref=stage.at[half, to], dst_ref=landing.at[half, mine[axis]],
-            send_sem=w_send.at[step, half, o - 1], recv_sem=w_recv.at[step, half, o - 1],
-            device_id={"dp": dest}, device_id_type=MESH,
-        )
-
-    w_copies = [[along(half, step, o) for o in (1, 3, 2) for half in range(2)] for step in range(2)]
-    for copy in w_copies[0]:
-        copy.start()
+            src_ref=stage.at[half, rest], dst_ref=landing.at[half, rest],
+            send_sem=w_send.at[step, half], recv_sem=w_recv.at[step, half],
+            device_id={"dp": lax.rem(me + 1, RANKS)}, device_id_type=MESH,
+        )
+
+    for e in range(SIDE):
+        for o in (1, 3, 2):
+            for half in range(2):
+                along(half, 0, o, e).start()
     for half in range(2):
         w_r[half, mine[half]] = w_s[half, mine[half]]
-    exchange(fill_dq, dq_s, dq_r, 4)
+    round_of(dq_s, dq_r, 4, 0, fill_dq)
 
     all_moved(dkv_s, dkv_r, 3).wait_recv()
     for j in range(NB):
@@ -395,24 +418,20 @@
         copy.start()
         z_copies.append(copy)
 
-    for copy in w_copies[0]:
-        copy.wait_recv()
+    for half in range(2):
+        all_along(half, 0).wait_recv()
     for half in range(2):
         for e in range(SIDE):
             total = jnp.zeros((WROWS, HD), F32)
             for r in range(SIDE):
                 total += w_r[half, r, e].astype(F32)
             w2_s[half, e] = total.astype(BF)
-    for copy in w_copies[1]:
-        copy.start()
+    for o in (1, 3, 2):
+        for half in range(2):
+            along(half, 1, o, 0).start()
     for half in range(2):
         w2_r[half, mine[1 - half]] = w2_s[half, mine[1 - half]]
-
-    all_moved(dq_s, dq_r, 4).wait_recv()
-    for j in range(NB):
-        q_v[j] = dq_r[homes[j]]
-    gq_out = pltpu.make_async_copy(q_v, gq_hbm, out_sem.at[0])
-    gq_out.start()
+    round_of(dq_s, dq_r, 4, 1, fill_dq)
 
     for copy in z_copies:
         copy.wait_recv()
@@ -428,8 +447,8 @@
             copy.start()
             copies.append(copy)
 
-    for copy in w_copies[1]:
-        copy.wait_recv()
+    for half in range(2):
+        all_along(half, 1).wait_recv()
     for half in range(2):
         total = jnp.zeros((WROWS, HD), F32)
         for r in range(SIDE):
@@ -438,12 +457,19 @@
     gw_out = pltpu.make_async_copy(gw_v, gw_hbm, out_sem.at[9])
     gw_out.start()
 
+    all_moved(dq_s, dq_r, 4).wait_recv()
+    for j in range(NB):
+        q_v[j] = dq_r[homes[j]]
+    gq_out = pltpu.make_async_copy(q_v, gq_hbm, out_sem.at[0])
+    gq_out.start()
+
     for kind, (stage, landing) in enumerate(
-        ((qkv_s, qkv_r), (ga_s, ga_r), (ao_s, ao_r), (dkv_s, dkv_r), (dq_s, dq_r))
+        ((q_s, q_r), (ga_s, ga_r), (ao_s, ao_r), (dkv_s, dkv_r), (dq_s, dq_r), (kv_s, kv_r))
     ):
         all_moved(stage, landing, kind).wait_send()
-    for copy in w_copies[0] + w_copies[1]:
-        copy.wait_send()
+    for half in range(2):
+        for step in range(2):
+            all_along(half, step).wait_send()
     share_kv.wait_send()
     share_dkv.wait_send()
     share_z.wait_send()
@@ -502,8 +528,10 @@
             V(blocked + (HD,), BF),
             V(blocked + (D,), BF),
             V((D, COLS), BF),
-            V((RANKS, RB, COLS + HD), BF),
-            V((RANKS, RB, COLS + HD), BF),
+            V((RANKS, RB, COLS), BF),
+            V((RANKS, RB, COLS), BF),
+            V((RANKS, RB, HD), BF),
+            V((RANKS, RB, HD), BF),
             V(blocked + (COLS,), BF),
             V((RANKS, RB, COLS), BF),
             V((RANKS, RB, COLS), BF),
@@ -536,14 +564,14 @@
             V(blocked + (RB,), jnp.int32),
             dma((3,)),
             dma((TILES,)),
-            dma((5,)),
-            dma((5,)),
+            dma((6,)),
+            dma((6,)),
             dma((3,)),
             dma((3,)),
             dma((3,)),
             dma((3,)),
-            dma((2, 2, 3)),
-            dma((2, 2, 3)),
+            dma((2, 2)),
+            dma((2, 2)),
             dma((10,)),
         ],
         compiler_params=pltpu.CompilerParams(

time: 89.5 us -> 84.3 us (0.942)
  Pallas kernels: 87.6 us -> 82.5 us
    pallas_call x1, Pallas kernels: 84.9 us -> 79.8 us  [local(): pl.pallas_call(kernel, out_shape=(jax.ShapeDtypeStruct(blocked + (COLS,),...]
where the time goes in v2:
time: 84.3 us; the launch traced here: 83.1 us
  Pallas kernels  82.5 us (98%)
    pallas_call x1, Pallas kernels, local(): pl.pallas_call(kernel, out_shape=(jax.ShapeDtypeStruct(blocked + (COLS,),...  79.8 us
    pallas_call x1, Pallas kernels, local(): pl.pallas_call(hand_on, out_shape=tuple((jax.ShapeDtypeStruct(x.shape, x....  2.65 us

profile of v2, /device:TPU:1, one launch (start us, length us, event | category | flops | bytes accessed | tf_op | source)
XLA Modules:
  0.0 83.1 jit_solution(16680669292360460640)
XLA Ops:
  0.6 79.8 %shard_map.111 = (bf16[8,128,256]{2,1,0:T(8,128)(2,1)}, bf16[8,128,512]{2,1,0:T(8,128)(2,1)}, bf16[8,128,512]{2,1,0:T(8,128)(2,1)}, f32[224,256]{1,0:T(8,128)}) custom-call(s32[128]{0:T(128)} %plan.1, s32[8,128]{1,0:T(8,128)} %bitcast.15, f32[8,128]{1,0:T(8,128)} %constant.2.clone.freq, bf16[8,128,256]{2,1,0:T(8,128)(2,1)} %bitcast.13, ...), custom_call_target="tpu_custom_call" | custom-call | flops 7000000000 | bytes 14680064 | tf_op jit(solution)/shard_map/pallas_call | solution.py:516
  80.4 2.6 %shard_map.112 = (bf16[8,128,256]{2,1,0:T(8,128)(2,1)}, bf16[8,128,512]{2,1,0:T(8,128)(2,1)}, bf16[8,128,512]{2,1,0:T(8,128)(2,1)}, f32[224,256]{1,0:T(8,128)}) custom-call(bf16[8,128,256]{2,1,0:T(8,128)(2,1)} %get-tuple-element.12.refs_0_, bf16[8,128,512]{2,1,0:T(8,128)(2,1)} %get-tuple-element.13.refs_1_, bf16[8,128,512]{2,1,0:T(8,128)(2,1)} %get-tuple-element.14.refs_2_, ...), custom_call_target="tpu_custom_call" | custom-call | tf_op jit(solution)/shard_map/pallas_call | solution.py:593

commit v3 on v2

--- a/solution.py
+++ b/solution.py
@@ -74,8 +74,8 @@
     gq_hbm, gk_hbm, gv_hbm, gw_hbm,
     q_v, kv_v, g_v, w_v, q_s, q_r, kv_s, kv_r, ga_v, ga_s, ga_r, kv2, qs, gas, outs, prob,
     ao_s, ao_r, dq_v, dq_s, dq_r, dkt, dvt, dkv_own, dkv_in, dkv_v, dkv_s, dkv_r,
-    w_s, w_r, w2_s, w2_r, zk, aoh, gw_v, cosf, sinf, start,
-    in_sem, g_sem, send_sem, recv_sem, pair_send, pair_recv, z_send, z_recv, w_send, w_recv, out_sem,
+    w_s, w_r, wn_r, wb_s, w2_s, w2_r, zk, aoh, gw_v, cosf, sinf, start,
+    in_sem, g_sem, send_sem, recv_sem, pair_send, pair_recv, z_send, z_recv, w_send, w_recv, w2_send, w2_recv, out_sem,
 ):
     me = lax.axis_index("dp")
     lane = lax.axis_index("tensor")
@@ -375,34 +375,44 @@
 
     mine = (my_x, my_y)
 
-    def along(half, step, o, e):
-        axis = half if step == 0 else 1 - half
-        to = lax.rem(mine[axis] + o, SIDE)
-        dest = to * SIDE + my_y if axis == 0 else my_x * SIDE + to
-        if step == 0:
-            src, dst = w_s.at[half, to, e], w_r.at[half, mine[axis], e]
-        else:
-            src, dst = w2_s.at[half, to], w2_r.at[half, mine[axis]]
+    def beside(axis, by):
+        to = lax.rem(mine[axis] + by, SIDE)
+        return to, (to * SIDE + my_y if axis == 0 else my_x * SIDE + to)
+
+    def near(kind, half, way):
+        to, dest = beside(half, (1, SIDE - 1)[way])
+        relayed, plain = pl.ds(2 * way, 2), pl.ds(2 - 2 * way, 2)
+        src, dst = (
+            (w_s.at[half, lax.rem(mine[half] + 2, SIDE), relayed], w_r.at[half, way]),
+            (w_s.at[half, to, plain], wn_r.at[half, way, plain]),
+            (wb_s.at[half, way], wn_r.at[half, way, relayed]),
+        )[kind]
         return pltpu.make_async_remote_copy(
-            src_ref=src, dst_ref=dst, send_sem=w_send.at[step, half], recv_sem=w_recv.at[step, half],
+            src_ref=src, dst_ref=dst,
+            send_sem=w_send.at[kind, half, way], recv_sem=w_recv.at[kind, half, way],
             device_id={"dp": dest}, device_id_type=MESH,
         )
 
-    def all_along(half, step):
-        stage, landing = ((w_s, w_r), (w2_s, w2_r))[step]
-        rest = pl.ds(0, SIDE - 1)
+    def last(half, o):
+        to, dest = beside(1 - half, o)
         return pltpu.make_async_remote_copy(
-            src_ref=stage.at[half, rest], dst_ref=landing.at[half, rest],
-            send_sem=w_send.at[step, half], recv_sem=w_recv.at[step, half],
-            device_id={"dp": lax.rem(me + 1, RANKS)}, device_id_type=MESH,
-        )
-
-    for e in range(SIDE):
-        for o in (1, 3, 2):
-            for half in range(2):
-                along(half, 0, o, e).start()
-    for half in range(2):
-        w_r[half, mine[half]] = w_s[half, mine[half]]
+            src_ref=w2_s.at[half, to], dst_ref=w2_r.at[half, mine[1 - half]],
+            send_sem=w2_send.at[half, o - 1], recv_sem=w2_recv.at[half, o - 1],
+            device_id={"dp": dest}, device_id_type=MESH,
+        )
+
+    ways = [(half, way) for way in range(2) for half in range(2)]
+    near_copies = [[near(kind, half, way) for half, way in ways] for kind in range(3)]
+    last_copies = [last(half, o) for o in (1, 3, 2) for half in range(2)]
+    for kind in range(2):
+        for copy in near_copies[kind]:
+            copy.start()
+    for i, (half, way) in enumerate(ways):
+        to, dest = beside(half, (1, SIDE - 1)[way])
+        near_copies[0][i].wait_recv()
+        both = w_r[half, way].astype(F32) + w_s[half, to, 2 * way : 2 * way + 2].astype(F32)
+        wb_s[half, way] = both.astype(BF)
+        near_copies[2][i].start()
     round_of(dq_s, dq_r, 4, 0, fill_dq)
 
     all_moved(dkv_s, dkv_r, 3).wait_recv()
@@ -418,17 +428,16 @@
         copy.start()
         z_copies.append(copy)
 
-    for half in range(2):
-        all_along(half, 0).wait_recv()
+    for copy in near_copies[1] + near_copies[2]:
+        copy.wait_recv()
     for half in range(2):
         for e in range(SIDE):
-            total = jnp.zeros((WROWS, HD), F32)
-            for r in range(SIDE):
-                total += w_r[half, r, e].astype(F32)
+            total = w_s[half, mine[half], e].astype(F32)
+            for way in range(2):
+                total += wn_r[half, way, e].astype(F32)
             w2_s[half, e] = total.astype(BF)
-    for o in (1, 3, 2):
-        for half in range(2):
-            along(half, 1, o, 0).start()
+    for copy in last_copies:
+        copy.start()
     for half in range(2):
         w2_r[half, mine[1 - half]] = w2_s[half, mine[1 - half]]
     round_of(dq_s, dq_r, 4, 1, fill_dq)
@@ -447,8 +456,8 @@
             copy.start()
             copies.append(copy)
 
-    for half in range(2):
-        all_along(half, 1).wait_recv()
+    for copy in last_copies:
+        copy.wait_recv()
     for half in range(2):
         total = jnp.zeros((WROWS, HD), F32)
         for r in range(SIDE):
@@ -467,9 +476,8 @@
         ((q_s, q_r), (ga_s, ga_r), (ao_s, ao_r), (dkv_s, dkv_r), (dq_s, dq_r), (kv_s, kv_r))
     ):
         all_moved(stage, landing, kind).wait_send()
-    for half in range(2):
-        for step in range(2):
-            all_along(half, step).wait_send()
+    for copy in near_copies[0] + near_copies[1] + near_copies[2] + last_copies:
+        copy.wait_send()
     share_kv.wait_send()
     share_dkv.wait_send()
     share_z.wait_send()
@@ -553,7 +561,9 @@
             V((RANKS, RB, HD), BF),
             V((RANKS, RB, HD), BF),
             V((2, SIDE, SIDE, WROWS, HD), BF),
-            V((2, SIDE, SIDE, WROWS, HD), BF),
+            V((2, 2, 2, WROWS, HD), BF),
+            V((2, 2, SIDE, WROWS, HD), BF),
+            V((2, 2, 2, WROWS, HD), BF),
             V((2, SIDE, WROWS, HD), BF),
             V((2, SIDE, WROWS, HD), BF),
             V((2, KV) + blocked + (HD,), BF),
@@ -570,8 +580,10 @@
             dma((3,)),
             dma((3,)),
             dma((3,)),
-            dma((2, 2)),
-            dma((2, 2)),
+            dma((3, 2, 2)),
+            dma((3, 2, 2)),
+            dma((2, 3)),
+            dma((2, 3)),
             dma((10,)),
         ],
         compiler_params=pltpu.CompilerParams(

time: 84.3 us -> 82.5 us (0.979); the launches traced: 83.1 us -> 82.3 us
  no operation moved by 1% of the time
where the time goes in v3:
time: 82.5 us; the launch traced here: 82.3 us
  Pallas kernels  81.7 us (99%)
    pallas_call x1, Pallas kernels, local(): pl.pallas_call(kernel, out_shape=(jax.ShapeDtypeStruct(blocked + (COLS,),...  79 us
    pallas_call x1, Pallas kernels, local(): pl.pallas_call(hand_on, out_shape=tuple((jax.ShapeDtypeStruct(x.shape, x....  2.65 us

profile of v3, /device:TPU:1, one launch (start us, length us, event | category | flops | bytes accessed | tf_op | source)
XLA Modules:
  0.0 82.3 jit_solution(15807303533887009071)
XLA Ops:
  0.6 79.0 %shard_map.111 = (bf16[8,128,256]{2,1,0:T(8,128)(2,1)}, bf16[8,128,512]{2,1,0:T(8,128)(2,1)}, bf16[8,128,512]{2,1,0:T(8,128)(2,1)}, f32[224,256]{1,0:T(8,128)}) custom-call(s32[128]{0:T(128)} %plan.1, s32[8,128]{1,0:T(8,128)} %bitcast.15, f32[8,128]{1,0:T(8,128)} %constant.2.clone.freq, bf16[8,128,256]{2,1,0:T(8,128)(2,1)} %bitcast.13, ...), custom_call_target="tpu_custom_call" | custom-call | flops 7000000000 | bytes 14680064 | tf_op jit(solution)/shard_map/pallas_call | solution.py:524
  79.7 2.6 %shard_map.112 = (bf16[8,128,256]{2,1,0:T(8,128)(2,1)}, bf16[8,128,512]{2,1,0:T(8,128)(2,1)}, bf16[8,128,512]{2,1,0:T(8,128)(2,1)}, f32[224,256]{1,0:T(8,128)}) custom-call(bf16[8,128,256]{2,1,0:T(8,128)(2,1)} %get-tuple-element.12.refs_0_, bf16[8,128,512]{2,1,0:T(8,128)(2,1)} %get-tuple-element.13.refs_1_, bf16[8,128,512]{2,1,0:T(8,128)(2,1)} %get-tuple-element.14.refs_2_, ...), custom_call_target="tpu_custom_call" | custom-call | tf_op jit(solution)/shard_map/pallas_call | solution.py:605

commit v4 on v3

--- a/solution.py
+++ b/solution.py
@@ -23,8 +23,8 @@
 WROWS = D // RANKS
 SIDE = 4
 ORDER = (
-    (1, 0), (0, 1), (3, 3), (2, 0), (0, 3), (1, 1), (3, 0), (0, 2),
-    (1, 3), (3, 1), (2, 2), (1, 2), (2, 3), (3, 2), (2, 1),
+    (2, 2), (1, 0), (0, 1), (1, 2), (3, 0), (0, 3), (2, 1), (1, 1),
+    (3, 2), (2, 0), (3, 3), (2, 3), (0, 2), (1, 3), (3, 1),
 )
 DX = sum(dx << (2 * i) for i, (dx, dy) in enumerate(ORDER))
 DY = sum(dy << (2 * i) for i, (dx, dy) in enumerate(ORDER))

time: 82.5 us -> 81.9 us (level)
  no operation moved by 1% of the time
where the time goes in v4:
time: 81.9 us; the launch traced here: 81.8 us
  Pallas kernels  81.1 us (99%)
    pallas_call x1, Pallas kernels, local(): pl.pallas_call(kernel, out_shape=(jax.ShapeDtypeStruct(blocked + (COLS,),...  78.5 us
    pallas_call x1, Pallas kernels, local(): pl.pallas_call(hand_on, out_shape=tuple((jax.ShapeDtypeStruct(x.shape, x....  2.65 us

profile of v4, /device:TPU:1, one launch (start us, length us, event | category | flops | bytes accessed | tf_op | source)
XLA Modules:
  0.0 81.8 jit_solution(13745969923448367031)
XLA Ops:
  0.6 78.5 %shard_map.111 = (bf16[8,128,256]{2,1,0:T(8,128)(2,1)}, bf16[8,128,512]{2,1,0:T(8,128)(2,1)}, bf16[8,128,512]{2,1,0:T(8,128)(2,1)}, f32[224,256]{1,0:T(8,128)}) custom-call(s32[128]{0:T(128)} %plan.1, s32[8,128]{1,0:T(8,128)} %bitcast.15, f32[8,128]{1,0:T(8,128)} %constant.2.clone.freq, bf16[8,128,256]{2,1,0:T(8,128)(2,1)} %bitcast.13, ...), custom_call_target="tpu_custom_call" | custom-call | flops 7000000000 | bytes 14680064 | tf_op jit(solution)/shard_map/pallas_call | solution.py:524
  79.1 2.6 %shard_map.112 = (bf16[8,128,256]{2,1,0:T(8,128)(2,1)}, bf16[8,128,512]{2,1,0:T(8,128)(2,1)}, bf16[8,128,512]{2,1,0:T(8,128)(2,1)}, f32[224,256]{1,0:T(8,128)}) custom-call(bf16[8,128,256]{2,1,0:T(8,128)(2,1)} %get-tuple-element.12.refs_0_, bf16[8,128,512]{2,1,0:T(8,128)(2,1)} %get-tuple-element.13.refs_1_, bf16[8,128,512]{2,1,0:T(8,128)(2,1)} %get-tuple-element.14.refs_2_, ...), custom_call_target="tpu_custom_call" | custom-call | tf_op jit(solution)/shard_map/pallas_call | solution.py:605

commit v5 on v4

--- a/solution.py
+++ b/solution.py
@@ -404,17 +404,10 @@
     ways = [(half, way) for way in range(2) for half in range(2)]
     near_copies = [[near(kind, half, way) for half, way in ways] for kind in range(3)]
     last_copies = [last(half, o) for o in (1, 3, 2) for half in range(2)]
-    for kind in range(2):
-        for copy in near_copies[kind]:
-            copy.start()
-    for i, (half, way) in enumerate(ways):
-        to, dest = beside(half, (1, SIDE - 1)[way])
-        near_copies[0][i].wait_recv()
-        both = w_r[half, way].astype(F32) + w_s[half, to, 2 * way : 2 * way + 2].astype(F32)
-        wb_s[half, way] = both.astype(BF)
-        near_copies[2][i].start()
-    round_of(dq_s, dq_r, 4, 0, fill_dq)
-
+    for copy in near_copies[0]:
+        copy.start()
+    for copy in near_copies[1]:
+        copy.start()
     all_moved(dkv_s, dkv_r, 3).wait_recv()
     for j in range(NB):
         zk[core, zed, j] = dkv_r[homes[j]]
@@ -427,6 +420,14 @@
         )
         copy.start()
         z_copies.append(copy)
+
+    for i, (half, way) in enumerate(ways):
+        to, dest = beside(half, (1, SIDE - 1)[way])
+        near_copies[0][i].wait_recv()
+        both = w_r[half, way].astype(F32) + w_s[half, to, 2 * way : 2 * way + 2].astype(F32)
+        wb_s[half, way] = both.astype(BF)
+        near_copies[2][i].start()
+    round_of(dq_s, dq_r, 4, 0, fill_dq)
 
     for copy in near_copies[1] + near_copies[2]:
         copy.wait_recv()

time: 81.9 us -> 81.3 us (level)
  Pallas kernels: 81.1 us -> 80.1 us
    pallas_call x1, Pallas kernels: 78.5 us -> 77.4 us  [local(): pl.pallas_call(kernel, out_shape=(jax.ShapeDtypeStruct(blocked + (COLS,),...]
where the time goes in v5:
time: 81.3 us; the launch traced here: 80.7 us
  Pallas kernels  80.1 us (99%)
    pallas_call x1, Pallas kernels, local(): pl.pallas_call(kernel, out_shape=(jax.ShapeDtypeStruct(blocked + (COLS,),...  77.4 us
    pallas_call x1, Pallas kernels, local(): pl.pallas_call(hand_on, out_shape=tuple((jax.ShapeDtypeStruct(x.shape, x....  2.65 us

profile of v5, /device:TPU:1, one launch (start us, length us, event | category | flops | bytes accessed | tf_op | source)
XLA Modules:
  0.0 80.7 jit_solution(14818280127748568548)
XLA Ops:
  0.6 77.4 %shard_map.111 = (bf16[8,128,256]{2,1,0:T(8,128)(2,1)}, bf16[8,128,512]{2,1,0:T(8,128)(2,1)}, bf16[8,128,512]{2,1,0:T(8,128)(2,1)}, f32[224,256]{1,0:T(8,128)}) custom-call(s32[128]{0:T(128)} %plan.1, s32[8,128]{1,0:T(8,128)} %bitcast.15, f32[8,128]{1,0:T(8,128)} %constant.2.clone.freq, bf16[8,128,256]{2,1,0:T(8,128)(2,1)} %bitcast.13, ...), custom_call_target="tpu_custom_call" | custom-call | flops 7000000000 | bytes 14680064 | tf_op jit(solution)/shard_map/pallas_call | solution.py:525
  78.1 2.6 %shard_map.112 = (bf16[8,128,256]{2,1,0:T(8,128)(2,1)}, bf16[8,128,512]{2,1,0:T(8,128)(2,1)}, bf16[8,128,512]{2,1,0:T(8,128)(2,1)}, f32[224,256]{1,0:T(8,128)}) custom-call(bf16[8,128,256]{2,1,0:T(8,128)(2,1)} %get-tuple-element.12.refs_0_, bf16[8,128,512]{2,1,0:T(8,128)(2,1)} %get-tuple-element.13.refs_1_, bf16[8,128,512]{2,1,0:T(8,128)(2,1)} %get-tuple-element.14.refs_2_, ...), custom_call_target="tpu_custom_call" | custom-call | tf_op jit(solution)/shard_map/pallas_call | solution.py:606

commit v6 on v5

--- a/solution.py
+++ b/solution.py
@@ -132,10 +132,10 @@
             slot = jnp.where((plan[me * NB + b] >> 3) == dest, b, slot)
         return slot
 
-    def moved(stage, landing, kind, dest, h):
+    def moved(stage, landing, kind, dest, first, count):
         return pltpu.make_async_remote_copy(
-            src_ref=stage.at[dest, pl.ds(64 * h, 64)],
-            dst_ref=landing.at[me, pl.ds(64 * h, 64)],
+            src_ref=stage.at[dest, pl.ds(first, count)],
+            dst_ref=landing.at[me, pl.ds(first, count)],
             send_sem=send_sem.at[kind],
             recv_sem=recv_sem.at[kind],
             device_id={"dp": dest},
@@ -153,24 +153,25 @@
             device_id_type=MESH,
         )
 
-    def round_of(stage, landing, kind, half, fill):
+    def round_of(stage, landing, kind, first, count, fill):
         def one(o, carry):
             dxs, dys = carry
             x = lax.rem(my_x + lax.rem(dxs, SIDE), SIDE)
             y = lax.rem(my_y + lax.rem(dys, SIDE), SIDE)
             dest = x * SIDE + y
-            if half == 0:
+            if first == 0:
                 fill(stage, dest, dest)
-            moved(stage, landing, kind, dest, half).start()
+            moved(stage, landing, kind, dest, first, count).start()
             return dxs // SIDE, dys // SIDE
 
         lax.fori_loop(1, RANKS, one, (DX + core * (DY - DX), DY + core * (DX - DY)))
-        if half == 0:
+        if first == 0:
             fill(landing, me, me)
 
-    def exchange(fill, stage, landing, kind):
-        for half in range(2):
-            round_of(stage, landing, kind, half, fill)
+    def exchange(fill, stage, landing, kind, rounds=2):
+        count = RB // rounds
+        for part in range(rounds):
+            round_of(stage, landing, kind, part * count, count, fill)
 
     pl.when(core == 0)(k_in.wait)
     pl.when(core == 1)(v_in.wait)
@@ -179,7 +180,7 @@
     def fill_kv(buffer, at, dest):
         buffer[at] = kv_v[send_slot(dest)]
 
-    exchange(fill_kv, kv_s, kv_r, 5)
+    exchange(fill_kv, kv_s, kv_r, 5, 1)
 
     q_in.wait()
 
@@ -359,7 +360,7 @@
     share_dkv.wait_recv()
     for b in range(NB):
         dkv_v[b] = (dkv_own[core, b].astype(F32) + dkv_in[b].astype(F32)).astype(BF)
-    exchange(fill_dkv, dkv_s, dkv_r, 3)
+    exchange(fill_dkv, dkv_s, dkv_r, 3, 1)
 
     all_moved(ao_s, ao_r, 2).wait_recv()
     for j in range(NB):
@@ -427,7 +428,7 @@
         both = w_r[half, way].astype(F32) + w_s[half, to, 2 * way : 2 * way + 2].astype(F32)
         wb_s[half, way] = both.astype(BF)
         near_copies[2][i].start()
-    round_of(dq_s, dq_r, 4, 0, fill_dq)
+    round_of(dq_s, dq_r, 4, 0, 64, fill_dq)
 
     for copy in near_copies[1] + near_copies[2]:
         copy.wait_recv()
@@ -441,7 +442,7 @@
         copy.start()
     for half in range(2):
         w2_r[half, mine[1 - half]] = w2_s[half, mine[1 - half]]
-    round_of(dq_s, dq_r, 4, 1, fill_dq)
+    round_of(dq_s, dq_r, 4, 64, 64, fill_dq)
 
     for copy in z_copies:
         copy.wait_recv()

time: 81.3 us -> 81.4 us (level)
  no operation moved by 1% of the time
where the time goes in v6:
time: 81.4 us; the launch traced here: 80 us
  Pallas kernels  79.4 us (98%)
    pallas_call x1, Pallas kernels, local(): pl.pallas_call(kernel, out_shape=(jax.ShapeDtypeStruct(blocked + (COLS,),...  76.8 us
    pallas_call x1, Pallas kernels, local(): pl.pallas_call(hand_on, out_shape=tuple((jax.ShapeDtypeStruct(x.shape, x....  2.65 us

profile of v6, /device:TPU:1, one launch (start us, length us, event | category | flops | bytes accessed | tf_op | source)
XLA Modules:
  0.0 80.0 jit_solution(226961029121107958)
XLA Ops:
  0.6 76.8 %shard_map.111 = (bf16[8,128,256]{2,1,0:T(8,128)(2,1)}, bf16[8,128,512]{2,1,0:T(8,128)(2,1)}, bf16[8,128,512]{2,1,0:T(8,128)(2,1)}, f32[224,256]{1,0:T(8,128)}) custom-call(s32[128]{0:T(128)} %plan.1, s32[8,128]{1,0:T(8,128)} %bitcast.15, f32[8,128]{1,0:T(8,128)} %constant.2.clone.freq, bf16[8,128,256]{2,1,0:T(8,128)(2,1)} %bitcast.13, ...), custom_call_target="tpu_custom_call" | custom-call | flops 7000000000 | bytes 14680064 | tf_op jit(solution)/shard_map/pallas_call | solution.py:526
  77.4 2.6 %shard_map.112 = (bf16[8,128,256]{2,1,0:T(8,128)(2,1)}, bf16[8,128,512]{2,1,0:T(8,128)(2,1)}, bf16[8,128,512]{2,1,0:T(8,128)(2,1)}, f32[224,256]{1,0:T(8,128)}) custom-call(bf16[8,128,256]{2,1,0:T(8,128)(2,1)} %get-tuple-element.12.refs_0_, bf16[8,128,512]{2,1,0:T(8,128)(2,1)} %get-tuple-element.13.refs_1_, bf16[8,128,512]{2,1,0:T(8,128)(2,1)} %get-tuple-element.14.refs_2_, ...), custom_call_target="tpu_custom_call" | custom-call | tf_op jit(solution)/shard_map/pallas_call | solution.py:607
